TPU v7x, 256 devices: a whole 4x4x8 slice. The times are simulated.
256 devices in a mesh: row: 64 (over x, z, core), col: 4 (over y).
Axes of the slice: x: 4, y: 4, z: 8, core: 2. Of those that a mesh axis runs over, the one named last changes fastest.
Arguments:
- right_side: bfloat16 [6, 128, 256, 512], P(None, 'row'), may hold values from -6 to 6
- lower_blocks: bfloat16 [5, 128, 8, 256, 256], P(None, 'row', None, 'col'), may hold values from -0.125 to 0.125
- upper_blocks: bfloat16 [5, 128, 8, 256, 256], P(None, 'row', None, 'col'), may hold values from -0.125 to 0.125
- lower_inverse: bfloat16 [6, 128, 256, 256], P(None, 'row', 'col'), may hold values from -0.3125 to 0.3125
- upper_inverse: bfloat16 [6, 128, 256, 256], P(None, 'row', 'col'), may hold values from -0.3125 to 0.3125
- lower_source: int32 [5, 128, 8], P(None, 'row'), may hold values from 0 to 127, as said below
- upper_source: int32 [5, 128, 8], P(None, 'row'), may hold values from 0 to 127, as said below
Outputs:
- solution: bfloat16 [6, 128, 256, 512], P(None, 'row', 'col')
Inputs may be any that keep to these rules, and one draw needn't show every extreme that they name: `lower_source`: each entry lies in the block of supernodes held by the same index of row as its own supernode n or by the index just before or after it: between max(0, (n // 2 - 1) * 2) and min(128, (n // 2 + 2) * 2) - 1. `upper_source`: each entry lies in the block of supernodes held by the same index of row as its own supernode n or by the index just before or after it: between max(0, (n // 2 - 1) * 2) and min(128, (n // 2 + 2) * 2) - 1.
All inputs are finite; a program needn't handle non-finite values.
Results may differ from a plain program's by a relative error of at most 0.04.
Values may be sent and summed in bfloat16 or wider, within the bound.
A program may use at most 64 MiB of HBM per device.

v0:
```python
import jax
import jax.numpy as jnp
from jax import lax
from jax.sharding import PartitionSpec as P


def with_halo(block, sides, width):
    for axis, dim in sides:
        count = lax.axis_size(axis)
        forward = [(i, i + 1) for i in range(count - 1)]
        backward = [(target, source) for source, target in forward]
        low = lax.ppermute(
            lax.slice_in_dim(block, block.shape[dim] - width, None, axis=dim), axis, forward
        )
        high = lax.ppermute(lax.slice_in_dim(block, 0, width, axis=dim), axis, backward)
        block = jnp.concatenate([low, block, high], axis=dim)
    return block


def contract(blocks, padded, sources, offset):
    local_index = sources - offset
    picked = padded[local_index]
    product = lax.dot_general(
        blocks, picked, (((1, 2), (1, 2)), ((0,), (0,))), preferred_element_type=jnp.float32
    )
    return product.astype(jnp.bfloat16)


def apply_inverse(inverse, values):
    return jnp.einsum("nij,njr->nir", inverse, values, preferred_element_type=jnp.float32).astype(
        jnp.bfloat16
    )


def on_device(
    right_side, lower_blocks, upper_blocks, lower_inverse, upper_inverse, lower_source, upper_source
):
    row_place = lax.axis_index("row")
    col_place = lax.axis_index("col")
    level_count = right_side.shape[0]
    node_count = right_side.shape[1]
    part_rows = lower_inverse.shape[2]
    offset = (row_place - 1) * node_count
    forward = [apply_inverse(lower_inverse[0], right_side[0])]
    for height in range(1, level_count):
        padded = with_halo(forward[-1], (("row", 0),), node_count)
        partial_value = contract(lower_blocks[height - 1], padded, lower_source[height - 1], offset)
        shares = lax.psum_scatter(partial_value, "col", scatter_dimension=1, tiled=True).astype(
            jnp.float32
        )
        own_rows = lax.dynamic_slice_in_dim(right_side[height], col_place * part_rows, part_rows, 1)
        remain_part = (own_rows.astype(jnp.float32) - shares).astype(jnp.bfloat16)
        remain = lax.all_gather(remain_part, "col", axis=1, tiled=True)
        forward.append(apply_inverse(lower_inverse[height], remain))
    top_whole = lax.all_gather(forward[level_count - 1], "col", axis=1, tiled=True)
    current = apply_inverse(upper_inverse[level_count - 1], top_whole)
    result = [current]
    for height in range(level_count - 2, -1, -1):
        padded = with_halo(current, (("row", 0),), node_count)
        partial_value = contract(upper_blocks[height], padded, upper_source[height], offset)
        shares = lax.psum_scatter(partial_value, "col", scatter_dimension=1, tiled=True).astype(
            jnp.float32
        )
        remain_part = (forward[height].astype(jnp.float32) - shares).astype(jnp.bfloat16)
        remain = lax.all_gather(remain_part, "col", axis=1, tiled=True)
        current = apply_inverse(upper_inverse[height], remain)
        result.append(current)
    return jnp.stack(result[::-1], axis=0)


def solution(mesh):
    placed = (
        P(None, "row", None, None),
        P(None, "row", None, "col", None),
        P(None, "row", None, "col", None),
        P(None, "row", "col", None),
        P(None, "row", "col", None),
        P(None, "row", None),
        P(None, "row", None),
    )
    return jax.shard_map(
        on_device,
        mesh=mesh,
        in_specs=placed,
        out_specs=P(None, "row", "col", None),
        check_vma=False,
    )
```

profile of v0, /device:TPU:2, one launch (start us, length us, event | category | flops | bytes accessed | tf_op | source)
XLA Modules:
  0.0 543.1 jit_solution(14333198824385333224)
XLA Ops:
  7.8 1.9 collective-permute-start
  9.8 7.2 %collective-permute-start.1 = (bf16[2,64,512]{2,1,0:T(8,128)(2,1)S(1)}, bf16[2,64,512]{2,1,0:T(8,128)(2,1)S(1)}, u32[]{:S(2)}, u32[]{:S(2)}) collective-permute-start(bf16[2,64,512]{2,1,0:T(8,128)(2,1)S(1)} %convolution_convert_fusion.11), channel_id=1, source_target_pairs={{4,0},{8,4},{12,8},{16,12},{20,16},{24,20},{28,24},{32,28},{36,32}... | collective-permute-start | bytes 393224 | tf_op jit(solution)/shard_map/ppermute | solution.py:15
  20.1 2.3 fusion.19
  22.5 2.7 fusion.78
  25.3 22.4 %reduce-scatter.11.cloned.1.call-done = bf16[2,64,512]{2,1,0:T(8,128)(2,1)} async-done(((bf16[2,256,512]{2,1,0:T(8,128)(2,1)}), bf16[2,64,512]{2,1,0:T(8,128)(2,1)}) %reduce-scatter.11.cloned.1.call-update) | async-done | bytes 131088 | tf_op jit(solution)/shard_map/reduce_scatter | solution.py:48
  48.6 12.8 %all_gather.33 = bf16[2,256,512]{2,1,0:T(8,128)(2,1)S(1)} all-gather(bf16[2,64,512]{2,1,0:T(8,128)(2,1)S(1)} %fusion.53), channel_id=1, replica_groups=mesh['row'=64,'col'=4] {'col'}, dimensions={1}, use_global_device_ids=true | all-gather | bytes 655360 | tf_op jit(solution)/shard_map/all_gather | solution.py:53
  62.5 1.9 collective-permute-start.2
  64.4 5.8 %collective-permute-start.3 = (bf16[2,64,512]{2,1,0:T(8,128)(2,1)S(1)}, bf16[2,64,512]{2,1,0:T(8,128)(2,1)S(1)}, u32[]{:S(2)}, u32[]{:S(2)}) collective-permute-start(bf16[2,64,512]{2,1,0:T(8,128)(2,1)S(1)} %fusion.20), channel_id=1, source_target_pairs={{4,0},{8,4},{12,8},{16,12},{20,16},{24,20},{28,24},{32,28},{36,32}... | collective-permute-start | bytes 393224 | tf_op jit(solution)/shard_map/ppermute | solution.py:15
  73.3 2.3 fusion.18
  75.7 23.4 %reduce-scatter.13.cloned.1.call-done = bf16[2,64,512]{2,1,0:T(8,128)(2,1)} async-done(((bf16[2,256,512]{2,1,0:T(8,128)(2,1)}), bf16[2,64,512]{2,1,0:T(8,128)(2,1)}) %reduce-scatter.13.cloned.1.call-update) | async-done | bytes 131088 | tf_op jit(solution)/shard_map/reduce_scatter | solution.py:48
  100.1 12.8 %all_gather.34 = bf16[2,256,512]{2,1,0:T(8,128)(2,1)S(1)} all-gather(bf16[2,64,512]{2,1,0:T(8,128)(2,1)S(1)} %fusion.52), channel_id=1, replica_groups=mesh['row'=64,'col'=4] {'col'}, dimensions={1}, use_global_device_ids=true | all-gather | bytes 655360 | tf_op jit(solution)/shard_map/all_gather | solution.py:53
  114.0 1.9 collective-permute-start.4
  115.9 5.8 %collective-permute-start.5 = (bf16[2,64,512]{2,1,0:T(8,128)(2,1)S(1)}, bf16[2,64,512]{2,1,0:T(8,128)(2,1)S(1)}, u32[]{:S(2)}, u32[]{:S(2)}) collective-permute-start(bf16[2,64,512]{2,1,0:T(8,128)(2,1)S(1)} %fusion.21), channel_id=1, source_target_pairs={{4,0},{8,4},{12,8},{16,12},{20,16},{24,20},{28,24},{32,28},{36,32}... | collective-permute-start | bytes 393224 | tf_op jit(solution)/shard_map/ppermute | solution.py:15
  124.8 2.3 fusion.17
  127.2 23.4 %reduce-scatter.15.cloned.1.call-done = bf16[2,64,512]{2,1,0:T(8,128)(2,1)} async-done(((bf16[2,256,512]{2,1,0:T(8,128)(2,1)}), bf16[2,64,512]{2,1,0:T(8,128)(2,1)}) %reduce-scatter.15.cloned.1.call-update) | async-done | bytes 131088 | tf_op jit(solution)/shard_map/reduce_scatter | solution.py:48
  151.6 12.8 %all_gather.35 = bf16[2,256,512]{2,1,0:T(8,128)(2,1)S(1)} all-gather(bf16[2,64,512]{2,1,0:T(8,128)(2,1)S(1)} %fusion.51), channel_id=1, replica_groups=mesh['row'=64,'col'=4] {'col'}, dimensions={1}, use_global_device_ids=true | all-gather | bytes 655360 | tf_op jit(solution)/shard_map/all_gather | solution.py:53
  165.4 1.9 collective-permute-start.6
  167.3 5.8 %collective-permute-start.7 = (bf16[2,64,512]{2,1,0:T(8,128)(2,1)S(1)}, bf16[2,64,512]{2,1,0:T(8,128)(2,1)S(1)}, u32[]{:S(2)}, u32[]{:S(2)}) collective-permute-start(bf16[2,64,512]{2,1,0:T(8,128)(2,1)S(1)} %fusion.22), channel_id=1, source_target_pairs={{4,0},{8,4},{12,8},{16,12},{20,16},{24,20},{28,24},{32,28},{36,32}... | collective-permute-start | bytes 393224 | tf_op jit(solution)/shard_map/ppermute | solution.py:15
  176.3 2.3 fusion.16
  178.7 23.4 %reduce-scatter.17.cloned.1.call-done = bf16[2,64,512]{2,1,0:T(8,128)(2,1)} async-done(((bf16[2,256,512]{2,1,0:T(8,128)(2,1)}), bf16[2,64,512]{2,1,0:T(8,128)(2,1)}) %reduce-scatter.17.cloned.1.call-update) | async-done | bytes 131088 | tf_op jit(solution)/shard_map/reduce_scatter | solution.py:48
  203.0 12.8 %all_gather.36 = bf16[2,256,512]{2,1,0:T(8,128)(2,1)S(1)} all-gather(bf16[2,64,512]{2,1,0:T(8,128)(2,1)S(1)} %fusion.50), channel_id=1, replica_groups=mesh['row'=64,'col'=4] {'col'}, dimensions={1}, use_global_device_ids=true | all-gather | bytes 655360 | tf_op jit(solution)/shard_map/all_gather | solution.py:53
  216.8 1.9 collective-permute-start.8
  218.8 5.8 %collective-permute-start.9 = (bf16[2,64,512]{2,1,0:T(8,128)(2,1)S(1)}, bf16[2,64,512]{2,1,0:T(8,128)(2,1)S(1)}, u32[]{:S(2)}, u32[]{:S(2)}) collective-permute-start(bf16[2,64,512]{2,1,0:T(8,128)(2,1)S(1)} %fusion.23), channel_id=1, source_target_pairs={{4,0},{8,4},{12,8},{16,12},{20,16},{24,20},{28,24},{32,28},{36,32}... | collective-permute-start | bytes 393224 | tf_op jit(solution)/shard_map/ppermute | solution.py:15
  227.7 2.4 fusion.15
  230.2 23.4 %reduce-scatter.19.cloned.1.call-done = bf16[2,64,512]{2,1,0:T(8,128)(2,1)} async-done(((bf16[2,256,512]{2,1,0:T(8,128)(2,1)}), bf16[2,64,512]{2,1,0:T(8,128)(2,1)}) %reduce-scatter.19.cloned.1.call-update) | async-done | bytes 131088 | tf_op jit(solution)/shard_map/reduce_scatter | solution.py:48
  254.5 12.8 %all_gather.37 = bf16[2,256,512]{2,1,0:T(8,128)(2,1)S(1)} all-gather(bf16[2,64,512]{2,1,0:T(8,128)(2,1)S(1)} %fusion.49), channel_id=1, replica_groups=mesh['row'=64,'col'=4] {'col'}, dimensions={1}, use_global_device_ids=true | all-gather | bytes 655360 | tf_op jit(solution)/shard_map/all_gather | solution.py:53
  268.4 13.2 %all_gather.38 = bf16[2,256,512]{2,1,0:T(8,128)(2,1)S(1)} all-gather(bf16[2,64,512]{2,1,0:T(8,128)(2,1)S(1)} %fusion.24), channel_id=1, replica_groups=mesh['row'=64,'col'=4] {'col'}, dimensions={1}, use_global_device_ids=true | all-gather | bytes 655360 | tf_op jit(solution)/shard_map/all_gather | solution.py:55
  281.7 1.9 collective-permute-start.10
  283.7 5.8 %collective-permute-start.11 = (bf16[2,64,512]{2,1,0:T(8,128)(2,1)S(1)}, bf16[2,64,512]{2,1,0:T(8,128)(2,1)S(1)}, u32[]{:S(2)}, u32[]{:S(2)}) collective-permute-start(bf16[2,64,512]{2,1,0:T(8,128)(2,1)S(1)} %bitcast.292), channel_id=1, source_target_pairs={{4,0},{8,4},{12,8},{16,12},{20,16},{24,20},{28,24},{32,28},{36,32}... | collective-permute-start | bytes 393224 | tf_op jit(solution)/shard_map/ppermute | solution.py:15
  292.6 2.3 fusion.14
  295.0 23.4 %reduce-scatter.21.cloned.1.call-done = bf16[2,64,512]{2,1,0:T(8,128)(2,1)} async-done(((bf16[2,256,512]{2,1,0:T(8,128)(2,1)}), bf16[2,64,512]{2,1,0:T(8,128)(2,1)}) %reduce-scatter.21.cloned.1.call-update) | async-done | bytes 131088 | tf_op jit(solution)/shard_map/reduce_scatter | solution.py:61
  319.3 12.8 %all_gather.39 = bf16[2,256,512]{2,1,0:T(8,128)(2,1)S(1)} all-gather(bf16[2,64,512]{2,1,0:T(8,128)(2,1)S(1)} %subtract_convert_fusion.4), channel_id=1, replica_groups=mesh['row'=64,'col'=4] {'col'}, dimensions={1}, use_global_device_ids=true | all-gather | bytes 655360 | tf_op jit(solution)/shard_map/all_gather | solution.py:65
  334.3 5.8 %collective-permute-start.13 = (bf16[2,64,512]{2,1,0:T(8,128)(2,1)S(1)}, bf16[2,64,512]{2,1,0:T(8,128)(2,1)S(1)}, u32[]{:S(2)}, u32[]{:S(2)}) collective-permute-start(bf16[2,64,512]{2,1,0:T(8,128)(2,1)S(1)} %bitcast.295), channel_id=1, source_target_pairs={{4,0},{8,4},{12,8},{16,12},{20,16},{24,20},{28,24},{32,28},{36,32}... | collective-permute-start | bytes 393224 | tf_op jit(solution)/shard_map/ppermute | solution.py:15
  343.2 2.3 fusion.13
  345.6 23.4 %reduce-scatter.23.cloned.1.call-done = bf16[2,64,512]{2,1,0:T(8,128)(2,1)} async-done(((bf16[2,256,512]{2,1,0:T(8,128)(2,1)}), bf16[2,64,512]{2,1,0:T(8,128)(2,1)}) %reduce-scatter.23.cloned.1.call-update) | async-done | bytes 131088 | tf_op jit(solution)/shard_map/reduce_scatter | solution.py:61
  369.9 12.8 %all_gather.40 = bf16[2,256,512]{2,1,0:T(8,128)(2,1)S(1)} all-gather(bf16[2,64,512]{2,1,0:T(8,128)(2,1)S(1)} %subtract_convert_fusion.3), channel_id=1, replica_groups=mesh['row'=64,'col'=4] {'col'}, dimensions={1}, use_global_device_ids=true | all-gather | bytes 655360 | tf_op jit(solution)/shard_map/all_gather | solution.py:65
  384.8 5.8 %collective-permute-start.15 = (bf16[2,64,512]{2,1,0:T(8,128)(2,1)S(1)}, bf16[2,64,512]{2,1,0:T(8,128)(2,1)S(1)}, u32[]{:S(2)}, u32[]{:S(2)}) collective-permute-start(bf16[2,64,512]{2,1,0:T(8,128)(2,1)S(1)} %bitcast.298), channel_id=1, source_target_pairs={{4,0},{8,4},{12,8},{16,12},{20,16},{24,20},{28,24},{32,28},{36,32}... | collective-permute-start | bytes 393224 | tf_op jit(solution)/shard_map/ppermute | solution.py:15
  393.8 2.3 fusion.12
  396.2 23.4 %reduce-scatter.25.cloned.1.call-done = bf16[2,64,512]{2,1,0:T(8,128)(2,1)} async-done(((bf16[2,256,512]{2,1,0:T(8,128)(2,1)}), bf16[2,64,512]{2,1,0:T(8,128)(2,1)}) %reduce-scatter.25.cloned.1.call-update) | async-done | bytes 131088 | tf_op jit(solution)/shard_map/reduce_scatter | solution.py:61
  420.5 12.8 %all_gather.41 = bf16[2,256,512]{2,1,0:T(8,128)(2,1)S(1)} all-gather(bf16[2,64,512]{2,1,0:T(8,128)(2,1)S(1)} %subtract_convert_fusion.2), channel_id=1, replica_groups=mesh['row'=64,'col'=4] {'col'}, dimensions={1}, use_global_device_ids=true | all-gather | bytes 655360 | tf_op jit(solution)/shard_map/all_gather | solution.py:65
  435.4 5.8 %collective-permute-start.17 = (bf16[2,64,512]{2,1,0:T(8,128)(2,1)S(1)}, bf16[2,64,512]{2,1,0:T(8,128)(2,1)S(1)}, u32[]{:S(2)}, u32[]{:S(2)}) collective-permute-start(bf16[2,64,512]{2,1,0:T(8,128)(2,1)S(1)} %bitcast.301), channel_id=1, source_target_pairs={{4,0},{8,4},{12,8},{16,12},{20,16},{24,20},{28,24},{32,28},{36,32}... | collective-permute-start | bytes 393224 | tf_op jit(solution)/shard_map/ppermute | solution.py:15
  444.4 2.3 fusion.11
  446.8 23.4 %reduce-scatter.27.cloned.1.call-done = bf16[2,64,512]{2,1,0:T(8,128)(2,1)} async-done(((bf16[2,256,512]{2,1,0:T(8,128)(2,1)}), bf16[2,64,512]{2,1,0:T(8,128)(2,1)}) %reduce-scatter.27.cloned.1.call-update) | async-done | bytes 131088 | tf_op jit(solution)/shard_map/reduce_scatter | solution.py:61
  471.1 12.8 %all_gather.42 = bf16[2,256,512]{2,1,0:T(8,128)(2,1)S(1)} all-gather(bf16[2,64,512]{2,1,0:T(8,128)(2,1)S(1)} %subtract_convert_fusion.1), channel_id=1, replica_groups=mesh['row'=64,'col'=4] {'col'}, dimensions={1}, use_global_device_ids=true | all-gather | bytes 655360 | tf_op jit(solution)/shard_map/all_gather | solution.py:65
  486.0 5.8 %collective-permute-start.19 = (bf16[2,64,512]{2,1,0:T(8,128)(2,1)S(1)}, bf16[2,64,512]{2,1,0:T(8,128)(2,1)S(1)}, u32[]{:S(2)}, u32[]{:S(2)}) collective-permute-start(bf16[2,64,512]{2,1,0:T(8,128)(2,1)S(1)} %bitcast.304), channel_id=1, source_target_pairs={{4,0},{8,4},{12,8},{16,12},{20,16},{24,20},{28,24},{32,28},{36,32}... | collective-permute-start | bytes 393224 | tf_op jit(solution)/shard_map/ppermute | solution.py:15
  494.9 2.3 fusion.10
  497.3 23.5 %reduce-scatter.29.cloned.1.call-done = bf16[2,64,512]{2,1,0:T(8,128)(2,1)} async-done(((bf16[2,256,512]{2,1,0:T(8,128)(2,1)}), bf16[2,64,512]{2,1,0:T(8,128)(2,1)}) %reduce-scatter.29.cloned.1.call-update) | async-done | bytes 131088 | tf_op jit(solution)/shard_map/reduce_scatter | solution.py:61
  521.7 12.8 %all_gather.43 = bf16[2,256,512]{2,1,0:T(8,128)(2,1)S(1)} all-gather(bf16[2,64,512]{2,1,0:T(8,128)(2,1)S(1)} %subtract_convert_fusion), channel_id=1, replica_groups=mesh['row'=64,'col'=4] {'col'}, dimensions={1}, use_global_device_ids=true | all-gather | bytes 655360 | tf_op jit(solution)/shard_map/all_gather | solution.py:65
  (126 shorter events, 58.5 us)
Async XLA Ops:
  6.5 41.1 %reduce-scatter.11.cloned.1.call-start = ((), (), s32[]{:S(2)}) async-start(), calls=%async_computation.10 | async-start | bytes 655360 | tf_op jit(solution)/shard_map/reduce_scatter | solution.py:48
  7.8 10.6 %collective-permute-start = (bf16[2,64,512]{2,1,0:T(8,128)(2,1)S(1)}, bf16[2,64,512]{2,1,0:T(8,128)(2,1)S(1)}, u32[]{:S(2)}, u32[]{:S(2)}) collective-permute-start(bf16[2,64,512]{2,1,0:T(8,128)(2,1)S(1)} %convolution_convert_fusion.11), channel_id=1, source_target_pairs={{0,4},{4,8},{8,12},{12,16},{16,20},{20,24},{24,28},{28,32},{32,36}... | collective-permute-start | bytes 393224 | tf_op jit(solution)/shard_map/ppermute | solution.py:12
  9.8 9.7 %collective-permute-start.1 = (bf16[2,64,512]{2,1,0:T(8,128)(2,1)S(1)}, bf16[2,64,512]{2,1,0:T(8,128)(2,1)S(1)}, u32[]{:S(2)}, u32[]{:S(2)}) collective-permute-start(bf16[2,64,512]{2,1,0:T(8,128)(2,1)S(1)} %convolution_convert_fusion.11), channel_id=1, source_target_pairs={{4,0},{8,4},{12,8},{16,12},{20,16},{24,20},{28,24},{32,28},{36,32}... | collective-permute-start | bytes 393224 | tf_op jit(solution)/shard_map/ppermute | solution.py:15
  22.5 76.7 %reduce-scatter.13.cloned.1.call-start = ((), (), s32[]{:S(2)}) async-start(), calls=%async_computation.11 | async-start | bytes 655360 | tf_op jit(solution)/shard_map/reduce_scatter | solution.py:48
  62.5 8.4 %collective-permute-start.2 = (bf16[2,64,512]{2,1,0:T(8,128)(2,1)S(1)}, bf16[2,64,512]{2,1,0:T(8,128)(2,1)S(1)}, u32[]{:S(2)}, u32[]{:S(2)}) collective-permute-start(bf16[2,64,512]{2,1,0:T(8,128)(2,1)S(1)} %fusion.20), channel_id=1, source_target_pairs={{0,4},{4,8},{8,12},{12,16},{16,20},{20,24},{24,28},{28,32},{32,36}... | collective-permute-start | bytes 393224 | tf_op jit(solution)/shard_map/ppermute | solution.py:12
  64.4 8.3 %collective-permute-start.3 = (bf16[2,64,512]{2,1,0:T(8,128)(2,1)S(1)}, bf16[2,64,512]{2,1,0:T(8,128)(2,1)S(1)}, u32[]{:S(2)}, u32[]{:S(2)}) collective-permute-start(bf16[2,64,512]{2,1,0:T(8,128)(2,1)S(1)} %fusion.20), channel_id=1, source_target_pairs={{4,0},{8,4},{12,8},{16,12},{20,16},{24,20},{28,24},{32,28},{36,32}... | collective-permute-start | bytes 393224 | tf_op jit(solution)/shard_map/ppermute | solution.py:15
  73.3 48.3 %copy-start.6 = (s32[2,8,1]{1,0,2:T(2,128)S(1)}, s32[2,8,1]{1,0,2:T(2,128)}, u32[]{:S(2)}) copy-start(s32[2,8,1]{1,0,2:T(2,128)} %get-tuple-element.23) | copy-start | bytes 196
  75.7 75.0 %reduce-scatter.15.cloned.1.call-start = ((), (), s32[]{:S(2)}) async-start(), calls=%async_computation.12 | async-start | bytes 655360 | tf_op jit(solution)/shard_map/reduce_scatter | solution.py:48
  114.0 8.4 %collective-permute-start.4 = (bf16[2,64,512]{2,1,0:T(8,128)(2,1)S(1)}, bf16[2,64,512]{2,1,0:T(8,128)(2,1)S(1)}, u32[]{:S(2)}, u32[]{:S(2)}) collective-permute-start(bf16[2,64,512]{2,1,0:T(8,128)(2,1)S(1)} %fusion.21), channel_id=1, source_target_pairs={{0,4},{4,8},{8,12},{12,16},{16,20},{20,24},{24,28},{28,32},{32,36}... | collective-permute-start | bytes 393224 | tf_op jit(solution)/shard_map/ppermute | solution.py:12
  115.9 8.3 %collective-permute-start.5 = (bf16[2,64,512]{2,1,0:T(8,128)(2,1)S(1)}, bf16[2,64,512]{2,1,0:T(8,128)(2,1)S(1)}, u32[]{:S(2)}, u32[]{:S(2)}) collective-permute-start(bf16[2,64,512]{2,1,0:T(8,128)(2,1)S(1)} %fusion.21), channel_id=1, source_target_pairs={{4,0},{8,4},{12,8},{16,12},{20,16},{24,20},{28,24},{32,28},{36,32}... | collective-permute-start | bytes 393224 | tf_op jit(solution)/shard_map/ppermute | solution.py:15
  124.8 48.3 %copy-start.5 = (s32[2,8,1]{1,0,2:T(2,128)S(1)}, s32[2,8,1]{1,0,2:T(2,128)}, u32[]{:S(2)}) copy-start(s32[2,8,1]{1,0,2:T(2,128)} %get-tuple-element.20) | copy-start | bytes 196
  127.2 74.9 %reduce-scatter.17.cloned.1.call-start = ((), (), s32[]{:S(2)}) async-start(), calls=%async_computation.13 | async-start | bytes 655360 | tf_op jit(solution)/shard_map/reduce_scatter | solution.py:48
  165.4 8.4 %collective-permute-start.6 = (bf16[2,64,512]{2,1,0:T(8,128)(2,1)S(1)}, bf16[2,64,512]{2,1,0:T(8,128)(2,1)S(1)}, u32[]{:S(2)}, u32[]{:S(2)}) collective-permute-start(bf16[2,64,512]{2,1,0:T(8,128)(2,1)S(1)} %fusion.22), channel_id=1, source_target_pairs={{0,4},{4,8},{8,12},{12,16},{16,20},{20,24},{24,28},{28,32},{32,36}... | collective-permute-start | bytes 393224 | tf_op jit(solution)/shard_map/ppermute | solution.py:12
  167.3 8.3 %collective-permute-start.7 = (bf16[2,64,512]{2,1,0:T(8,128)(2,1)S(1)}, bf16[2,64,512]{2,1,0:T(8,128)(2,1)S(1)}, u32[]{:S(2)}, u32[]{:S(2)}) collective-permute-start(bf16[2,64,512]{2,1,0:T(8,128)(2,1)S(1)} %fusion.22), channel_id=1, source_target_pairs={{4,0},{8,4},{12,8},{16,12},{20,16},{24,20},{28,24},{32,28},{36,32}... | collective-permute-start | bytes 393224 | tf_op jit(solution)/shard_map/ppermute | solution.py:15
  176.3 48.3 %copy-start.4 = (s32[2,8,1]{1,0,2:T(2,128)S(1)}, s32[2,8,1]{1,0,2:T(2,128)}, u32[]{:S(2)}) copy-start(s32[2,8,1]{1,0,2:T(2,128)} %get-tuple-element.24) | copy-start | bytes 196
  178.6 74.9 %reduce-scatter.19.cloned.1.call-start = ((), (), s32[]{:S(2)}) async-start(), calls=%async_computation.14 | async-start | bytes 655360 | tf_op jit(solution)/shard_map/reduce_scatter | solution.py:48
  216.8 8.4 %collective-permute-start.8 = (bf16[2,64,512]{2,1,0:T(8,128)(2,1)S(1)}, bf16[2,64,512]{2,1,0:T(8,128)(2,1)S(1)}, u32[]{:S(2)}, u32[]{:S(2)}) collective-permute-start(bf16[2,64,512]{2,1,0:T(8,128)(2,1)S(1)} %fusion.23), channel_id=1, source_target_pairs={{0,4},{4,8},{8,12},{12,16},{16,20},{20,24},{24,28},{28,32},{32,36}... | collective-permute-start | bytes 393224 | tf_op jit(solution)/shard_map/ppermute | solution.py:12
  218.8 8.3 %collective-permute-start.9 = (bf16[2,64,512]{2,1,0:T(8,128)(2,1)S(1)}, bf16[2,64,512]{2,1,0:T(8,128)(2,1)S(1)}, u32[]{:S(2)}, u32[]{:S(2)}) collective-permute-start(bf16[2,64,512]{2,1,0:T(8,128)(2,1)S(1)} %fusion.23), channel_id=1, source_target_pairs={{4,0},{8,4},{12,8},{16,12},{20,16},{24,20},{28,24},{32,28},{36,32}... | collective-permute-start | bytes 393224 | tf_op jit(solution)/shard_map/ppermute | solution.py:15
  227.7 53.8 %copy-start = (bf16[6,2,64,256]{3,2,1,0:T(8,128)(2,1)S(1)}, bf16[6,2,64,256]{3,2,1,0:T(8,128)(2,1)}, u32[]{:S(2)}) copy-start(bf16[6,2,64,256]{3,2,1,0:T(8,128)(2,1)} %param.11) | copy-start | bytes 1179652
  227.7 61.7 %copy-start.3 = (s32[2,8,1]{1,0,2:T(2,128)S(1)}, s32[2,8,1]{1,0,2:T(2,128)}, u32[]{:S(2)}) copy-start(s32[2,8,1]{1,0,2:T(2,128)} %get-tuple-element.13) | copy-start | bytes 196
  230.1 88.3 %reduce-scatter.21.cloned.1.call-start = ((), (), s32[]{:S(2)}) async-start(), calls=%async_computation.15 | async-start | bytes 655360 | tf_op jit(solution)/shard_map/reduce_scatter | solution.py:61
  281.7 8.4 %collective-permute-start.10 = (bf16[2,64,512]{2,1,0:T(8,128)(2,1)S(1)}, bf16[2,64,512]{2,1,0:T(8,128)(2,1)S(1)}, u32[]{:S(2)}, u32[]{:S(2)}) collective-permute-start(bf16[2,64,512]{2,1,0:T(8,128)(2,1)S(1)} %bitcast.291), channel_id=1, source_target_pairs={{0,4},{4,8},{8,12},{12,16},{16,20},{20,24},{24,28},{28,32},{32,36}... | collective-permute-start | bytes 393224 | tf_op jit(solution)/shard_map/ppermute | solution.py:12
  283.7 8.3 %collective-permute-start.11 = (bf16[2,64,512]{2,1,0:T(8,128)(2,1)S(1)}, bf16[2,64,512]{2,1,0:T(8,128)(2,1)S(1)}, u32[]{:S(2)}, u32[]{:S(2)}) collective-permute-start(bf16[2,64,512]{2,1,0:T(8,128)(2,1)S(1)} %bitcast.292), channel_id=1, source_target_pairs={{4,0},{8,4},{12,8},{16,12},{20,16},{24,20},{28,24},{32,28},{36,32}... | collective-permute-start | bytes 393224 | tf_op jit(solution)/shard_map/ppermute | solution.py:15
  292.6 47.4 %copy-start.2 = (s32[2,8,1]{1,0,2:T(2,128)S(1)}, s32[2,8,1]{1,0,2:T(2,128)}, u32[]{:S(2)}) copy-start(s32[2,8,1]{1,0,2:T(2,128)} %get-tuple-element.12) | copy-start | bytes 196
  295.0 74.0 %reduce-scatter.23.cloned.1.call-start = ((), (), s32[]{:S(2)}) async-start(), calls=%async_computation.16 | async-start | bytes 655360 | tf_op jit(solution)/shard_map/reduce_scatter | solution.py:61
  332.3 8.4 %collective-permute-start.12 = (bf16[2,64,512]{2,1,0:T(8,128)(2,1)S(1)}, bf16[2,64,512]{2,1,0:T(8,128)(2,1)S(1)}, u32[]{:S(2)}, u32[]{:S(2)}) collective-permute-start(bf16[2,64,512]{2,1,0:T(8,128)(2,1)S(1)} %bitcast.294), channel_id=1, source_target_pairs={{0,4},{4,8},{8,12},{12,16},{16,20},{20,24},{24,28},{28,32},{32,36}... | collective-permute-start | bytes 393224 | tf_op jit(solution)/shard_map/ppermute | solution.py:12
  334.3 8.3 %collective-permute-start.13 = (bf16[2,64,512]{2,1,0:T(8,128)(2,1)S(1)}, bf16[2,64,512]{2,1,0:T(8,128)(2,1)S(1)}, u32[]{:S(2)}, u32[]{:S(2)}) collective-permute-start(bf16[2,64,512]{2,1,0:T(8,128)(2,1)S(1)} %bitcast.295), channel_id=1, source_target_pairs={{4,0},{8,4},{12,8},{16,12},{20,16},{24,20},{28,24},{32,28},{36,32}... | collective-permute-start | bytes 393224 | tf_op jit(solution)/shard_map/ppermute | solution.py:15
  345.5 74.0 %reduce-scatter.25.cloned.1.call-start = ((), (), s32[]{:S(2)}) async-start(), calls=%async_computation.17 | async-start | bytes 655360 | tf_op jit(solution)/shard_map/reduce_scatter | solution.py:61
  382.9 8.4 %collective-permute-start.14 = (bf16[2,64,512]{2,1,0:T(8,128)(2,1)S(1)}, bf16[2,64,512]{2,1,0:T(8,128)(2,1)S(1)}, u32[]{:S(2)}, u32[]{:S(2)}) collective-permute-start(bf16[2,64,512]{2,1,0:T(8,128)(2,1)S(1)} %bitcast.297), channel_id=1, source_target_pairs={{0,4},{4,8},{8,12},{12,16},{16,20},{20,24},{24,28},{28,32},{32,36}... | collective-permute-start | bytes 393224 | tf_op jit(solution)/shard_map/ppermute | solution.py:12
  384.8 8.3 %collective-permute-start.15 = (bf16[2,64,512]{2,1,0:T(8,128)(2,1)S(1)}, bf16[2,64,512]{2,1,0:T(8,128)(2,1)S(1)}, u32[]{:S(2)}, u32[]{:S(2)}) collective-permute-start(bf16[2,64,512]{2,1,0:T(8,128)(2,1)S(1)} %bitcast.298), channel_id=1, source_target_pairs={{4,0},{8,4},{12,8},{16,12},{20,16},{24,20},{28,24},{32,28},{36,32}... | collective-permute-start | bytes 393224 | tf_op jit(solution)/shard_map/ppermute | solution.py:15
  396.1 74.0 %reduce-scatter.27.cloned.1.call-start = ((), (), s32[]{:S(2)}) async-start(), calls=%async_computation.18 | async-start | bytes 655360 | tf_op jit(solution)/shard_map/reduce_scatter | solution.py:61
  433.5 8.4 %collective-permute-start.16 = (bf16[2,64,512]{2,1,0:T(8,128)(2,1)S(1)}, bf16[2,64,512]{2,1,0:T(8,128)(2,1)S(1)}, u32[]{:S(2)}, u32[]{:S(2)}) collective-permute-start(bf16[2,64,512]{2,1,0:T(8,128)(2,1)S(1)} %bitcast.300), channel_id=1, source_target_pairs={{0,4},{4,8},{8,12},{12,16},{16,20},{20,24},{24,28},{28,32},{32,36}... | collective-permute-start | bytes 393224 | tf_op jit(solution)/shard_map/ppermute | solution.py:12
  435.4 8.3 %collective-permute-start.17 = (bf16[2,64,512]{2,1,0:T(8,128)(2,1)S(1)}, bf16[2,64,512]{2,1,0:T(8,128)(2,1)S(1)}, u32[]{:S(2)}, u32[]{:S(2)}) collective-permute-start(bf16[2,64,512]{2,1,0:T(8,128)(2,1)S(1)} %bitcast.301), channel_id=1, source_target_pairs={{4,0},{8,4},{12,8},{16,12},{20,16},{24,20},{28,24},{32,28},{36,32}... | collective-permute-start | bytes 393224 | tf_op jit(solution)/shard_map/ppermute | solution.py:15
  446.7 74.0 %reduce-scatter.29.cloned.1.call-start = ((), (), s32[]{:S(2)}) async-start(), calls=%async_computation.19 | async-start | bytes 655360 | tf_op jit(solution)/shard_map/reduce_scatter | solution.py:61
  484.1 8.4 %collective-permute-start.18 = (bf16[2,64,512]{2,1,0:T(8,128)(2,1)S(1)}, bf16[2,64,512]{2,1,0:T(8,128)(2,1)S(1)}, u32[]{:S(2)}, u32[]{:S(2)}) collective-permute-start(bf16[2,64,512]{2,1,0:T(8,128)(2,1)S(1)} %bitcast.303), channel_id=1, source_target_pairs={{0,4},{4,8},{8,12},{12,16},{16,20},{20,24},{24,28},{28,32},{32,36}... | collective-permute-start | bytes 393224 | tf_op jit(solution)/shard_map/ppermute | solution.py:12
  486.0 8.3 %collective-permute-start.19 = (bf16[2,64,512]{2,1,0:T(8,128)(2,1)S(1)}, bf16[2,64,512]{2,1,0:T(8,128)(2,1)S(1)}, u32[]{:S(2)}, u32[]{:S(2)}) collective-permute-start(bf16[2,64,512]{2,1,0:T(8,128)(2,1)S(1)} %bitcast.304), channel_id=1, source_target_pairs={{4,0},{8,4},{12,8},{16,12},{20,16},{24,20},{28,24},{32,28},{36,32}... | collective-permute-start | bytes 393224 | tf_op jit(solution)/shard_map/ppermute | solution.py:15
  534.8 0.9 copy-start.1
Sparse Core Ops, SparseCore 0:
  22.6 25.0 reduce-scatter.10
  75.8 23.2 reduce-scatter.12
  127.3 23.2 reduce-scatter.14
  178.8 23.2 reduce-scatter.16
  230.2 23.2 reduce-scatter.18
  295.1 23.2 reduce-scatter.20
  345.7 23.2 reduce-scatter.22
  396.2 23.2 reduce-scatter.24
  446.8 23.2 reduce-scatter.26
  497.4 23.3 reduce-scatter.28
where the time goes:
time: 545 us; the launch traced here: 543 us
  waiting for transfers between devices  256 us (47%)
  blocking collectives  141 us (26%)
  starting transfers between devices  78.5 us (14%)
  matrix products  31 us (6%)
  between operations  14.1 us (3%)
  other arithmetic  11.4 us (2%)
  local copies, waits for them, and re-layouts  11.3 us (2%)
    reduce_scatter x10, waiting for transfers between devices, on_device(): lax.psum_scatter(partial_value, 'col', scatter_dimension=1, tiled=True)  233 us
    all_gather x10, blocking collectives, on_device(): remain = lax.all_gather(remain_part, 'col', axis=1, tiled=True)  128 us
    ppermute x10, starting transfers between devices, with_halo(): lax.ppermute(lax.slice_in_dim(block, 0, width, axis=dim), axis, backward)  58.9 us
    dot_general x10, matrix products, contract(): lax.dot_general(blocks, picked, (((1, 2), (1, 2)), ((0,), (0,))), preferr...  23.3 us
    ppermute x10, starting transfers between devices, with_halo(): lax.ppermute(lax.slice_in_dim(block, block.shape[dim] - width, None, axis...  19.2 us
    ppermute x10, waiting for transfers between devices, with_halo(): lax.ppermute(lax.slice_in_dim(block, 0, width, axis=dim), axis, backward)  17.1 us
    all_gather x1, blocking collectives, on_device(): lax.all_gather(forward[level_count - 1], 'col', axis=1, tiled=True)  13.2 us
  transfers between devices with their start and end apart: 30, of which 29 were waited for; matrix products, arithmetic and copies ran while one was open for 1% of the time, Pallas kernels for 0%

commit v1 on v0

v1 whole, which is shorter than its diff:
```python
import functools

import jax
import jax.numpy as jnp
from jax import lax
from jax.experimental import pallas as pl
from jax.experimental.pallas import tpu as pltpu
from jax.sharding import PartitionSpec as P

BF16 = jnp.bfloat16
F32 = jnp.float32
CHUNKS = 2


def dot(left, right):
    return lax.dot_general(left, right, (((1,), (0,)), ((), ())), preferred_element_type=F32)


def dot_nt(left, right):
    return lax.dot_general(left, right, (((1,), (1,)), ((), ())), preferred_element_type=F32)


def kernel(
    sizes,
    right_side,
    lower_blocks,
    upper_blocks,
    lower_inverse,
    upper_inverse,
    lower_source,
    upper_source,
    out,
    first_inverse,
    first_side,
    blocks,
    inverse,
    gathered,
    operator,
    known,
    kept,
    sent,
    received,
    halo_out,
    halo_in,
    part_out,
    part_in,
    gather_out,
    gather_in,
    first_sem,
    block_sem,
    own_sem,
    extra_sem,
    result_sem,
):
    levels, nodes, terms, part, order, rows, columns = sizes
    steps = 2 * (levels - 1)
    top = levels - 2
    wide = columns // CHUNKS
    row = lax.axis_index("row")
    col = lax.axis_index("col")
    count = lax.axis_size("row")
    ring = lax.axis_size("col")
    has_low = row > 0
    has_high = row < count - 1
    low = (row - 1, col)
    high = (row + 1, col)
    after = (row, lax.rem(col + 1, ring))
    before = (row, lax.rem(col + ring - 1, ring))
    own_rows = pl.ds(pl.multiple_of(col * part, part), part)

    load_inverse = pltpu.make_async_copy(lower_inverse.at[0], first_inverse, first_sem.at[0])
    load_side = pltpu.make_async_copy(right_side.at[0], first_side, first_sem.at[1])

    def load_blocks(step, source, level):
        return pltpu.make_async_copy(source.at[level], blocks.at[step], block_sem.at[step])

    def load_own(turn, source, level):
        return pltpu.make_async_copy(source.at[level], gathered.at[turn, :, 0], own_sem.at[turn])

    def load_extra(step, chunk):
        return pltpu.make_async_copy(
            right_side.at[step + 1, :, own_rows, pl.ds(chunk * wide, wide)],
            known.at[step, chunk, pl.ds(3 * nodes, nodes)],
            extra_sem.at[step, chunk],
        )

    all_blocks = [load_blocks(s, lower_blocks, s) for s in range(levels - 1)]
    all_blocks += [load_blocks(s, upper_blocks, steps - 1 - s) for s in range(levels - 1, steps)]
    all_own = [load_own(t, lower_inverse, t + 1) for t in range(levels - 1)]
    all_own += [load_own(t, upper_inverse, steps - t) for t in range(levels - 1, steps + 1)]
    all_extra = [load_extra(s, h) for s in range(levels - 1) for h in range(CHUNKS)]

    all_own[0].start()
    load_inverse.start()
    load_side.start()
    all_blocks[0].start()
    for copy in all_own[1:3]:
        copy.start()
    for copy in all_extra[:CHUNKS]:
        copy.start()
    all_blocks[1].start()

    barrier = pltpu.get_barrier_semaphore()
    for place in (after, before):
        pl.semaphore_signal(barrier, inc=1, device_id=place, device_id_type=pl.DeviceIdType.MESH)

    @pl.when(has_low)
    def _():
        pl.semaphore_signal(barrier, inc=1, device_id=low, device_id_type=pl.DeviceIdType.MESH)

    @pl.when(has_high)
    def _():
        pl.semaphore_signal(barrier, inc=1, device_id=high, device_id_type=pl.DeviceIdType.MESH)

    for copy in all_own[3:]:
        copy.start()
    for copy in all_extra[CHUNKS:]:
        copy.start()
    for copy in all_blocks[2:]:
        copy.start()

    line = lax.broadcasted_iota(jnp.int32, (part, order), 0)
    place = lax.broadcasted_iota(jnp.int32, (part, order), 1)
    chosen = jnp.where(place == line + col * part, 1.0, 0.0).astype(BF16)
    for node in range(nodes):
        for other in range(nodes):
            operator_rows = chosen if node == other else jnp.zeros((part, order), BF16)
            inverse[node, 3 * nodes + other] = operator_rows

    @pl.when(jnp.logical_not(has_low))
    def _():
        known[:, :, 0:nodes] = jnp.zeros((steps + 1, CHUNKS, nodes, part, wide), BF16)

    @pl.when(jnp.logical_not(has_high))
    def _():
        known[:, :, 2 * nodes : 3 * nodes] = jnp.zeros((steps + 1, CHUNKS, nodes, part, wide), BF16)

    pl.semaphore_wait(barrier, 2 + jnp.where(has_low, 1, 0) + jnp.where(has_high, 1, 0))

    def remote(source, target, out_sem, in_sem, place):
        return pltpu.make_async_remote_copy(
            src_ref=source,
            dst_ref=target,
            send_sem=out_sem,
            recv_sem=in_sem,
            device_id=place,
            device_id_type=pl.DeviceIdType.MESH,
        )

    def gather_copy(turn, which):
        source, target, place = (
            (gathered.at[turn, :, 0], gathered.at[turn, :, 3], after),
            (gathered.at[turn, :, 0], gathered.at[turn, :, 1], before),
            (gathered.at[turn, 0, 3], gathered.at[turn, 0, 2], after),
            (gathered.at[turn, 1, 1], gathered.at[turn, 1, 2], before),
        )[which]
        return remote(source, target, gather_out.at[turn, which], gather_in.at[turn, which], place)

    def halo_copy(step, chunk, side):
        source = known.at[step, chunk, pl.ds(nodes, nodes)]
        target = known.at[step, chunk, pl.ds(0 if side == 0 else 2 * nodes, nodes)]
        return remote(
            source,
            target,
            halo_out.at[step, chunk, side],
            halo_in.at[step, chunk, side],
            high if side == 0 else low,
        )

    def part_copy(step, chunk, which):
        return remote(
            sent.at[step, chunk, which],
            received.at[step, chunk, which],
            part_out.at[step, chunk, which],
            part_in.at[step, chunk, which],
            after if which % 2 == 0 else before,
        )

    def result_copy(step, chunk):
        return pltpu.make_async_copy(
            known.at[step + 1, chunk, pl.ds(nodes, nodes)],
            out.at[steps - 1 - step, :, :, pl.ds(chunk * wide, wide)],
            result_sem.at[step, chunk],
        )

    def start_gather(turn):
        pltpu.make_async_copy(
            lower_inverse.at[0], gathered.at[turn, :, 0], own_sem.at[turn]
        ).wait()
        gather_copy(turn, 0).start()
        gather_copy(turn, 1).start()

    def relay_gather(turn):
        gather_copy(turn, 0).wait_recv()
        gather_copy(turn, 2).start()
        gather_copy(turn, 1).wait_recv()
        gather_copy(turn, 3).start()

    def end_gather(turn):
        gather_copy(turn, 2).wait_recv()
        gather_copy(turn, 3).wait_recv()

    def start_halo(step, chunk):
        @pl.when(has_high)
        def _():
            halo_copy(step, chunk, 0).start()

        @pl.when(has_low)
        def _():
            halo_copy(step, chunk, 1).start()

    def end_halo(step, chunk):
        @pl.when(has_low)
        def _():
            halo_copy(step, chunk, 0).wait_recv()

        @pl.when(has_high)
        def _():
            halo_copy(step, chunk, 1).wait_recv()

    def sum_blocks(step):
        pltpu.make_async_copy(lower_blocks.at[0], blocks.at[step], block_sem.at[step]).wait()
        is_lower = step < levels - 1
        lower_level = jnp.minimum(step, levels - 2)
        upper_level = jnp.minimum(steps - 1 - step, levels - 2)
        base = (row - 1) * nodes
        tile = 16

        def one(node):
            slots = []
            for term in range(terms):
                source = jnp.where(
                    is_lower,
                    lower_source[lower_level, node, term],
                    upper_source[upper_level, node, term],
                )
                slots.append(source - base)
            for start in range(0, part, tile):
                values = [
                    blocks[step, node, term, start : start + tile, :].astype(F32)
                    for term in range(terms)
                ]
                for slot in range(3 * nodes):
                    total = jnp.zeros((tile, order), F32)
                    for term in range(terms):
                        total = total - jnp.where(slots[term] == slot, values[term], 0.0)
                    inverse[node, slot, start : start + tile, :] = total.astype(BF16)

        for node in range(nodes):
            one(node)

    def make_operator(step):
        sum_blocks(step)
        turn = step + jnp.where(step < levels - 1, 0, 1)

        @pl.when(step == top)
        def _():
            end_gather(top)
            end_gather(top + 1)
            for node in range(nodes):
                lower = jnp.concatenate(
                    [gathered[top, node, lax.rem(a - col + ring, ring)] for a in range(4)], axis=0
                )
                upper = gathered[top + 1, node].reshape(order, order)
                both = dot(upper, lower).astype(BF16)
                blocks_of = inverse[node].reshape(4 * nodes * part, order)
                operator[step, :, node] = (
                    dot_nt(both, blocks_of).astype(BF16).reshape(4, part, 4 * nodes * part)
                )

        @pl.when(step != top)
        def _():
            end_gather(turn)
            for node in range(nodes):
                blocks_of = inverse[node].reshape(4 * nodes * part, order)
                operator[step, :, node] = (
                    dot_nt(gathered[turn, node].reshape(order, order), blocks_of)
                    .astype(BF16)
                    .reshape(4, part, 4 * nodes * part)
                )

    def multiply(step, chunk):
        @pl.when(step < levels - 1)
        def _():
            pltpu.make_async_copy(
                right_side.at[1, :, own_rows, pl.ds(chunk * wide, wide)],
                known.at[step, chunk, pl.ds(3 * nodes, nodes)],
                extra_sem.at[jnp.minimum(step, levels - 2), chunk],
            ).wait()

        end_halo(step, chunk)
        values = known[step, chunk].reshape(4 * nodes * part, wide)
        far = dot(operator[step, 2].reshape(nodes * part, -1), values)
        sent[step, chunk, 0] = far[:part].astype(BF16)
        sent[step, chunk, 1] = far[part:].astype(BF16)
        part_copy(step, chunk, 0).start()
        part_copy(step, chunk, 1).start()
        near = dot(operator[step, 1].reshape(nodes * part, -1), values)
        sent[step, chunk, 2] = near[part:].astype(BF16)
        part_copy(step, chunk, 2).start()
        kept[chunk, 0] = near[:part]
        near = dot(operator[step, 3].reshape(nodes * part, -1), values)
        sent[step, chunk, 3] = near[:part].astype(BF16)
        part_copy(step, chunk, 3).start()
        kept[chunk, 1] = near[part:]
        own = dot(operator[step, 0].reshape(nodes * part, -1), values)
        kept[chunk, 2] = own[:part]
        kept[chunk, 3] = own[part:]

    def pass_on(step, chunk):
        for which in range(2):
            part_copy(step, chunk, which).wait_recv()
            sent[step, chunk, 4 + which] = (
                kept[chunk, which] + received[step, chunk, which].astype(F32)
            ).astype(BF16)
            part_copy(step, chunk, 4 + which).start()

    def finish(step, chunk):
        for which in (2, 3, 4, 5):
            part_copy(step, chunk, which).wait_recv()
        first = kept[chunk, 2] + received[step, chunk, 3].astype(F32)
        first = (first + received[step, chunk, 4].astype(F32)).astype(BF16)
        second = kept[chunk, 3] + received[step, chunk, 2].astype(F32)
        second = (second + received[step, chunk, 5].astype(F32)).astype(BF16)
        known[step + 1, chunk, nodes] = first
        known[step + 1, chunk, nodes + 1] = second

        @pl.when(step < steps - 1)
        def _():
            start_halo(step + 1, chunk)

        @pl.when(step < top)
        def _():
            known[steps - 2 - step, chunk, 3 * nodes] = first
            known[steps - 2 - step, chunk, 3 * nodes + 1] = second

        @pl.when(step >= top)
        def _():
            result_copy(step, chunk).start()

    start_gather(0)
    load_inverse.wait()
    load_side.wait()
    for chunk in range(CHUNKS):
        for node in range(nodes):
            value = dot(
                first_inverse[node], first_side[node, :, chunk * wide : (chunk + 1) * wide]
            ).astype(BF16)
            known[0, chunk, nodes + node] = value
            known[steps - 1, chunk, 3 * nodes + node] = value
        start_halo(0, chunk)
    relay_gather(0)
    start_gather(1)
    make_operator(0)

    def body(step, carry):
        multiply(step, 0)

        @pl.when(step > 0)
        def _():
            finish(step - 1, 1)

        @pl.when(step == 0)
        def _():
            relay_gather(1)
            start_gather(2)
            start_gather(3)

        @pl.when(step < steps - 1)
        def _():
            make_operator(step + 1)

        pass_on(step, 0)
        multiply(step, 1)
        finish(step, 0)

        @pl.when(step == 0)
        def _():
            relay_gather(2)

        @pl.when(step + 4 <= steps)
        def _():
            start_gather(step + 4)

        pass_on(step, 1)

        @pl.when(step + 3 <= steps)
        def _():
            relay_gather(step + 3)

        return carry

    for step in range(steps):
        body(step, 0)
    finish(steps - 1, 1)

    def drain(step, carry):
        for chunk in range(CHUNKS):
            for which in range(6):
                part_copy(step, chunk, which).wait_send()

            @pl.when(has_high)
            def _():
                halo_copy(step, chunk, 0).wait_send()

            @pl.when(has_low)
            def _():
                halo_copy(step, chunk, 1).wait_send()

            @pl.when(step >= top)
            def _():
                result_copy(step, chunk).wait()

        return carry

    lax.fori_loop(0, steps, drain, 0)

    def drain_gather(turn, carry):
        for which in range(4):
            gather_copy(turn, which).wait_send()
        return carry

    lax.fori_loop(0, steps + 1, drain_gather, 0)


def on_device(
    right_side, lower_blocks, upper_blocks, lower_inverse, upper_inverse, lower_source, upper_source
):
    levels, nodes, order, columns = right_side.shape
    terms, part = lower_blocks.shape[2:4]
    rows = nodes * part
    steps = 2 * (levels - 1)
    wide = columns // CHUNKS
    sizes = (levels, nodes, terms, part, order, rows, columns)
    anywhere = pl.BlockSpec(memory_space=pl.ANY)
    scalars = pl.BlockSpec(memory_space=pltpu.SMEM)
    dma = pltpu.SemaphoreType.DMA
    return pl.pallas_call(
        functools.partial(kernel, sizes),
        out_shape=jax.ShapeDtypeStruct((levels, nodes, part, columns), BF16),
        in_specs=[anywhere] * 5 + [scalars] * 2,
        out_specs=anywhere,
        scratch_shapes=[
            pltpu.VMEM((nodes, part, order), BF16),
            pltpu.VMEM((nodes, order, columns), BF16),
            pltpu.VMEM((steps, nodes, terms, part, order), BF16),
            pltpu.VMEM((nodes, 4 * nodes, part, order), BF16),
            pltpu.VMEM((steps + 1, nodes, 4, part, order), BF16),
            pltpu.VMEM((steps, 4, nodes, part, 4 * nodes * part), BF16),
            pltpu.VMEM((steps + 1, CHUNKS, 4 * nodes, part, wide), BF16),
            pltpu.VMEM((CHUNKS, 4, part, wide), F32),
            pltpu.VMEM((steps, CHUNKS, 6, part, wide), BF16),
            pltpu.VMEM((steps, CHUNKS, 6, part, wide), BF16),
            dma((steps + 1, CHUNKS, 2)),
            dma((steps + 1, CHUNKS, 2)),
            dma((steps, CHUNKS, 6)),
            dma((steps, CHUNKS, 6)),
            dma((steps + 1, 4)),
            dma((steps + 1, 4)),
            dma((2,)),
            dma((steps,)),
            dma((steps + 1,)),
            dma((levels - 1, CHUNKS)),
            dma((steps, CHUNKS)),
        ],
        compiler_params=pltpu.CompilerParams(
            collective_id=0, has_side_effects=True, vmem_limit_bytes=48 * 1024 * 1024
        ),
        cost_estimate=pl.CostEstimate(
            flops=4_000_000_000, bytes_accessed=10_000_000, transcendentals=0
        ),
        name="solve",
    )(
        right_side,
        lower_blocks,
        upper_blocks,
        lower_inverse,
        upper_inverse,
        lower_source,
        upper_source,
    )


def solution(mesh):
    placed = (
        P(None, "row", None, None),
        P(None, "row", None, "col", None),
        P(None, "row", None, "col", None),
        P(None, "row", "col", None),
        P(None, "row", "col", None),
        P(None, "row", None),
        P(None, "row", None),
    )
    return jax.shard_map(
        on_device,
        mesh=mesh,
        in_specs=placed,
        out_specs=P(None, "row", "col", None),
        check_vma=False,
    )
```

time: 545 us -> 134 us (0.25)
  waiting for transfers between devices: 256 us -> 0 us
  blocking collectives: 141 us -> 0 us
  Pallas kernels: 0 us -> 128 us
  starting transfers between devices: 78.5 us -> 0 us
  matrix products: 31 us -> 0 us
  between operations: 14.1 us -> 0.01 us
  other arithmetic: 11.4 us -> 0 us
    reduce_scatter x10 -> x0, waiting for transfers between devices: 233 us -> none  [on_device(): lax.psum_scatter(partial_value, 'col', scatter_dimension=1, tiled=True)]
    all_gather x11 -> x0, blocking collectives: 141 us -> none  [the longest x10 128 us: on_device(): remain = lax.all_gather(remain_part, 'col', axis=1, tiled=True)]
    pallas_call x0 -> x1, Pallas kernels: none -> 128 us  [on_device(): pl.pallas_call(functools.partial(kernel, sizes), out_shape=jax.ShapeDtype...]
    ppermute x20 -> x0, starting transfers between devices: 78.1 us -> none  [the longest x10 58.9 us: with_halo(): lax.ppermute(lax.slice_in_dim(block, 0, width, axis=dim), axis, backward)]
    dot_general x22 -> x0, matrix products: 31 us -> none  [the longest x10 23.3 us: contract(): lax.dot_general(blocks, picked, (((1, 2), (1, 2)), ((0,), (0,))), preferr...]
    ppermute x20 -> x0, waiting for transfers between devices: 22.6 us -> none  [the longest x10 17.1 us: with_halo(): lax.ppermute(lax.slice_in_dim(block, 0, width, axis=dim), axis, backward)]
    convert_element_type x10 -> x0, other arithmetic: 9.43 us -> none  [the longest x5 4.75 us: on_device(): remain_part = (own_rows.astype(jnp.float32) - shares).astype(jnp.bfloat16)]
    gather x10 -> x0, local copies, waits for them, and re-layouts: 6.14 us -> none  [contract(): picked = padded[local_index]]
  transfers between devices with their start and end apart: 30 -> 0, of which waited for: 29 -> 0; matrix products, arithmetic and copies ran while one was open for 1% -> 0% of each run, Pallas kernels for 0% -> 0%
where the time goes in v1:
time: 134 us
  Pallas kernels  128 us (96%)
  local copies, waits for them, and re-layouts  5.99 us (4%)
    pallas_call x1, Pallas kernels, on_device(): pl.pallas_call(functools.partial(kernel, sizes), out_shape=jax.ShapeDtype...  128 us
    unnamed x11, local copies, waits for them, and re-layouts  5.99 us

profile of v1, /device:TPU:2, one launch (start us, length us, event | category | flops | bytes accessed | tf_op | source)
XLA Modules:
  0.0 133.7 jit_solution(16618387225047948454)
XLA Ops:
  0.0 0.0 copy-start
  0.0 1.7 %copy-done = bf16[5,2,8,64,256]{4,3,2,1,0:T(8,128)(2,1)S(1)} copy-done((bf16[5,2,8,64,256]{4,3,2,1,0:T(8,128)(2,1)S(1)}, bf16[5,2,8,64,256]{4,3,2,1,0:T(8,128)(2,1)}, u32[]{:S(2)}) %copy-start) | copy-done | bytes 2621464
  1.7 0.0 copy-start.1
  1.7 1.0 copy-done.1
  2.7 0.0 copy-start.2
  2.7 1.0 copy-done.2
  3.7 0.0 copy-start.3
  3.7 0.7 copy-done.3
  4.4 0.0 copy-start.4
  4.4 0.7 copy-done.4
  5.1 127.7 %solve.1 = bf16[6,2,64,512]{3,2,1,0:T(8,128)(2,1)S(1)} custom-call(bf16[6,2,256,512]{3,2,1,0:T(8,128)(2,1)} %right_side.1, bf16[5,2,8,64,256]{4,3,2,1,0:T(8,128)(2,1)S(1)} %copy-done, bf16[5,2,8,64,256]{4,3,2,1,0:T(8,128)(2,1)} %upper_blocks.1, bf16[6,2,64,256]{3,2,1,0:T(8,128)(2,1)S(1)} %copy-done.1, bf16[6,2,64,256]{3,2,1,0:T(8,128)(2,1)S(1)} %copy-done.2, ...), custom_call_target="tpu_custom_call" | custom-call | flops 4000000000 | bytes 10000000 | tf_op jit(solution)/shard_map/solve/pallas_call | solution.py:438
  132.8 0.9 copy.9
Async XLA Ops:
  0.0 1.7 %copy-start = (bf16[5,2,8,64,256]{4,3,2,1,0:T(8,128)(2,1)S(1)}, bf16[5,2,8,64,256]{4,3,2,1,0:T(8,128)(2,1)}, u32[]{:S(2)}) copy-start(bf16[5,2,8,64,256]{4,3,2,1,0:T(8,128)(2,1)} %lower_blocks.1) | copy-start | bytes 7864324
  1.7 1.0 copy-start.1
  2.7 1.0 copy-start.2
  3.7 0.7 copy-start.3
  4.4 0.7 copy-start.4

commit v2 on v1

--- a/solution.py
+++ b/solution.py
@@ -9,7 +9,8 @@
 
 BF16 = jnp.bfloat16
 F32 = jnp.float32
-CHUNKS = 2
+CHUNKS = 4
+DIRECT = 2
 
 
 def dot(left, right):
@@ -66,6 +67,8 @@
     high = (row + 1, col)
     after = (row, lax.rem(col + 1, ring))
     before = (row, lax.rem(col + ring - 1, ring))
+    across = (row, lax.rem(col + 2, ring))
+    peers = (across, after, before)
     own_rows = pl.ds(pl.multiple_of(col * part, part), part)
 
     load_inverse = pltpu.make_async_copy(lower_inverse.at[0], first_inverse, first_sem.at[0])
@@ -75,7 +78,7 @@
         return pltpu.make_async_copy(source.at[level], blocks.at[step], block_sem.at[step])
 
     def load_own(turn, source, level):
-        return pltpu.make_async_copy(source.at[level], gathered.at[turn, :, 0], own_sem.at[turn])
+        return pltpu.make_async_copy(source.at[level], gathered.at[turn, :, 3], own_sem.at[turn])
 
     def load_extra(step, chunk):
         return pltpu.make_async_copy(
@@ -101,7 +104,7 @@
     all_blocks[1].start()
 
     barrier = pltpu.get_barrier_semaphore()
-    for place in (after, before):
+    for place in peers:
         pl.semaphore_signal(barrier, inc=1, device_id=place, device_id_type=pl.DeviceIdType.MESH)
 
     @pl.when(has_low)
@@ -135,7 +138,7 @@
     def _():
         known[:, :, 2 * nodes : 3 * nodes] = jnp.zeros((steps + 1, CHUNKS, nodes, part, wide), BF16)
 
-    pl.semaphore_wait(barrier, 2 + jnp.where(has_low, 1, 0) + jnp.where(has_high, 1, 0))
+    pl.semaphore_wait(barrier, 3 + jnp.where(has_low, 1, 0) + jnp.where(has_high, 1, 0))
 
     def remote(source, target, out_sem, in_sem, place):
         return pltpu.make_async_remote_copy(
@@ -149,10 +152,11 @@
 
     def gather_copy(turn, which):
         source, target, place = (
-            (gathered.at[turn, :, 0], gathered.at[turn, :, 3], after),
-            (gathered.at[turn, :, 0], gathered.at[turn, :, 1], before),
-            (gathered.at[turn, 0, 3], gathered.at[turn, 0, 2], after),
-            (gathered.at[turn, 1, 1], gathered.at[turn, 1, 2], before),
+            (gathered.at[turn, :, 3], gathered.at[turn, :, 2], after),
+            (gathered.at[turn, :, 3], gathered.at[turn, :, 1], before),
+            (gathered.at[turn, 0, 2], gathered.at[turn, 0, 0], after),
+            (gathered.at[turn, 1, 1], gathered.at[turn, 1, 0], before),
+            (gathered.at[turn, :, 3], gathered.at[turn, :, 0], across),
         )[which]
         return remote(source, target, gather_out.at[turn, which], gather_in.at[turn, which], place)
 
@@ -173,7 +177,7 @@
             received.at[step, chunk, which],
             part_out.at[step, chunk, which],
             part_in.at[step, chunk, which],
-            after if which % 2 == 0 else before,
+            peers[which],
         )
 
     def result_copy(step, chunk):
@@ -185,20 +189,24 @@
 
     def start_gather(turn):
         pltpu.make_async_copy(
-            lower_inverse.at[0], gathered.at[turn, :, 0], own_sem.at[turn]
+            lower_inverse.at[0], gathered.at[turn, :, 3], own_sem.at[turn]
         ).wait()
+        if turn < DIRECT:
+            gather_copy(turn, 4).start()
         gather_copy(turn, 0).start()
         gather_copy(turn, 1).start()
 
     def relay_gather(turn):
+        if turn < DIRECT:
+            return
         gather_copy(turn, 0).wait_recv()
         gather_copy(turn, 2).start()
         gather_copy(turn, 1).wait_recv()
         gather_copy(turn, 3).start()
 
     def end_gather(turn):
-        gather_copy(turn, 2).wait_recv()
-        gather_copy(turn, 3).wait_recv()
+        for which in (0, 1, 4) if turn < DIRECT else (2, 3):
+            gather_copy(turn, which).wait_recv()
 
     def start_halo(step, chunk):
         @pl.when(has_high)
@@ -221,20 +229,15 @@
     def sum_blocks(step):
         pltpu.make_async_copy(lower_blocks.at[0], blocks.at[step], block_sem.at[step]).wait()
         is_lower = step < levels - 1
-        lower_level = jnp.minimum(step, levels - 2)
-        upper_level = jnp.minimum(steps - 1 - step, levels - 2)
+        sources = lower_source if is_lower else upper_source
+        level = step if is_lower else steps - 1 - step
         base = (row - 1) * nodes
         tile = 16
 
         def one(node):
             slots = []
             for term in range(terms):
-                source = jnp.where(
-                    is_lower,
-                    lower_source[lower_level, node, term],
-                    upper_source[upper_level, node, term],
-                )
-                slots.append(source - base)
+                slots.append(sources[level, node, term] - base)
             for start in range(0, part, tile):
                 values = [
                     blocks[step, node, term, start : start + tile, :].astype(F32)
@@ -251,91 +254,54 @@
 
     def make_operator(step):
         sum_blocks(step)
-        turn = step + jnp.where(step < levels - 1, 0, 1)
-
-        @pl.when(step == top)
-        def _():
-            end_gather(top)
+        turn = step if step < levels - 1 else step + 1
+        end_gather(turn)
+        if step == top:
             end_gather(top + 1)
-            for node in range(nodes):
-                lower = jnp.concatenate(
-                    [gathered[top, node, lax.rem(a - col + ring, ring)] for a in range(4)], axis=0
-                )
+        for node in range(nodes):
+            left = gathered[turn, node].reshape(order, order)
+            if step == top:
+                places = [lax.rem(a - col + ring, ring) for a in range(4)]
+                slots = [
+                    jnp.where(p == 0, 3, jnp.where(p == 1, 1, jnp.where(p == 2, 0, 2)))
+                    for p in places
+                ]
+                lower = jnp.concatenate([gathered[top, node, p] for p in slots], axis=0)
                 upper = gathered[top + 1, node].reshape(order, order)
-                both = dot(upper, lower).astype(BF16)
-                blocks_of = inverse[node].reshape(4 * nodes * part, order)
-                operator[step, :, node] = (
-                    dot_nt(both, blocks_of).astype(BF16).reshape(4, part, 4 * nodes * part)
-                )
-
-        @pl.when(step != top)
-        def _():
-            end_gather(turn)
-            for node in range(nodes):
-                blocks_of = inverse[node].reshape(4 * nodes * part, order)
-                operator[step, :, node] = (
-                    dot_nt(gathered[turn, node].reshape(order, order), blocks_of)
-                    .astype(BF16)
-                    .reshape(4, part, 4 * nodes * part)
-                )
+                left = dot(upper, lower).astype(BF16)
+            right = inverse[node].reshape(4 * nodes * part, order)
+            operator[step, :, node] = (
+                dot_nt(left, right).astype(BF16).reshape(4, part, 4 * nodes * part)
+            )
 
     def multiply(step, chunk):
-        @pl.when(step < levels - 1)
-        def _():
-            pltpu.make_async_copy(
-                right_side.at[1, :, own_rows, pl.ds(chunk * wide, wide)],
-                known.at[step, chunk, pl.ds(3 * nodes, nodes)],
-                extra_sem.at[jnp.minimum(step, levels - 2), chunk],
-            ).wait()
-
+        if step < levels - 1:
+            load_extra(step, chunk).wait()
         end_halo(step, chunk)
         values = known[step, chunk].reshape(4 * nodes * part, wide)
-        far = dot(operator[step, 2].reshape(nodes * part, -1), values)
-        sent[step, chunk, 0] = far[:part].astype(BF16)
-        sent[step, chunk, 1] = far[part:].astype(BF16)
+        half = 2 * nodes * part
+        one = dot(operator[step, 0:2].reshape(half, -1), values)
+        sent[step, chunk, 0:2] = one.astype(BF16).reshape(2, nodes, part, wide)
         part_copy(step, chunk, 0).start()
         part_copy(step, chunk, 1).start()
-        near = dot(operator[step, 1].reshape(nodes * part, -1), values)
-        sent[step, chunk, 2] = near[part:].astype(BF16)
+        two = dot(operator[step, 2:4].reshape(half, -1), values)
+        sent[step, chunk, 2] = two[: nodes * part].astype(BF16).reshape(nodes, part, wide)
         part_copy(step, chunk, 2).start()
-        kept[chunk, 0] = near[:part]
-        near = dot(operator[step, 3].reshape(nodes * part, -1), values)
-        sent[step, chunk, 3] = near[:part].astype(BF16)
-        part_copy(step, chunk, 3).start()
-        kept[chunk, 1] = near[part:]
-        own = dot(operator[step, 0].reshape(nodes * part, -1), values)
-        kept[chunk, 2] = own[:part]
-        kept[chunk, 3] = own[part:]
-
-    def pass_on(step, chunk):
-        for which in range(2):
+        kept[chunk] = two[nodes * part :].reshape(nodes, part, wide)
+
+    def finish(step, chunk):
+        total = kept[chunk]
+        for which in (1, 2, 0):
             part_copy(step, chunk, which).wait_recv()
-            sent[step, chunk, 4 + which] = (
-                kept[chunk, which] + received[step, chunk, which].astype(F32)
-            ).astype(BF16)
-            part_copy(step, chunk, 4 + which).start()
-
-    def finish(step, chunk):
-        for which in (2, 3, 4, 5):
-            part_copy(step, chunk, which).wait_recv()
-        first = kept[chunk, 2] + received[step, chunk, 3].astype(F32)
-        first = (first + received[step, chunk, 4].astype(F32)).astype(BF16)
-        second = kept[chunk, 3] + received[step, chunk, 2].astype(F32)
-        second = (second + received[step, chunk, 5].astype(F32)).astype(BF16)
-        known[step + 1, chunk, nodes] = first
-        known[step + 1, chunk, nodes + 1] = second
-
-        @pl.when(step < steps - 1)
-        def _():
+        for which in range(3):
+            total = total + received[step, chunk, which].astype(F32)
+        value = total.astype(BF16)
+        known[step + 1, chunk, nodes : 2 * nodes] = value
+        if step < steps - 1:
             start_halo(step + 1, chunk)
-
-        @pl.when(step < top)
-        def _():
-            known[steps - 2 - step, chunk, 3 * nodes] = first
-            known[steps - 2 - step, chunk, 3 * nodes + 1] = second
-
-        @pl.when(step >= top)
-        def _():
+        if step < top:
+            known[steps - 2 - step, chunk, 3 * nodes :] = value
+        if step >= top:
             result_copy(step, chunk).start()
 
     start_gather(0)
@@ -353,74 +319,51 @@
     start_gather(1)
     make_operator(0)
 
-    def body(step, carry):
-        multiply(step, 0)
-
-        @pl.when(step > 0)
-        def _():
-            finish(step - 1, 1)
-
-        @pl.when(step == 0)
-        def _():
-            relay_gather(1)
-            start_gather(2)
-            start_gather(3)
-
-        @pl.when(step < steps - 1)
-        def _():
-            make_operator(step + 1)
-
-        pass_on(step, 0)
-        multiply(step, 1)
-        finish(step, 0)
-
-        @pl.when(step == 0)
-        def _():
-            relay_gather(2)
-
-        @pl.when(step + 4 <= steps)
-        def _():
+    late = CHUNKS // 2
+    for step in range(steps):
+        for chunk in range(CHUNKS):
+            multiply(step, chunk)
+            if chunk < late:
+                if step > 0:
+                    finish(step - 1, late + chunk)
+            else:
+                finish(step, chunk - late)
+            if chunk == 0 and step == 0:
+                start_gather(2)
+                start_gather(3)
+            if chunk == late - 1 and step < steps - 1:
+                make_operator(step + 1)
+            if chunk == late and step + 3 <= steps:
+                relay_gather(step + 3)
+                if step == 0:
+                    relay_gather(2)
+        if step + 4 <= steps:
             start_gather(step + 4)
-
-        pass_on(step, 1)
-
-        @pl.when(step + 3 <= steps)
-        def _():
-            relay_gather(step + 3)
-
-        return carry
+    for chunk in range(late, CHUNKS):
+        finish(steps - 1, chunk)
 
     for step in range(steps):
-        body(step, 0)
-    finish(steps - 1, 1)
-
-    def drain(step, carry):
         for chunk in range(CHUNKS):
-            for which in range(6):
+            for which in range(3):
                 part_copy(step, chunk, which).wait_send()
-
-            @pl.when(has_high)
-            def _():
+            if step >= top:
+                result_copy(step, chunk).wait()
+
+    @pl.when(has_high)
+    def _():
+        for step in range(steps):
+            for chunk in range(CHUNKS):
                 halo_copy(step, chunk, 0).wait_send()
 
-            @pl.when(has_low)
-            def _():
+    @pl.when(has_low)
+    def _():
+        for step in range(steps):
+            for chunk in range(CHUNKS):
                 halo_copy(step, chunk, 1).wait_send()
 
-            @pl.when(step >= top)
-            def _():
-                result_copy(step, chunk).wait()
-
-        return carry
-
-    lax.fori_loop(0, steps, drain, 0)
-
-    def drain_gather(turn, carry):
-        for which in range(4):
+    for turn in range(steps + 1):
+        for which in (0, 1, 4) if turn < DIRECT else (0, 1, 2, 3):
             gather_copy(turn, which).wait_send()
-        return carry
-
-    lax.fori_loop(0, steps + 1, drain_gather, 0)
 
 
 def on_device(
@@ -448,15 +391,15 @@
             pltpu.VMEM((steps + 1, nodes, 4, part, order), BF16),
             pltpu.VMEM((steps, 4, nodes, part, 4 * nodes * part), BF16),
             pltpu.VMEM((steps + 1, CHUNKS, 4 * nodes, part, wide), BF16),
-            pltpu.VMEM((CHUNKS, 4, part, wide), F32),
-            pltpu.VMEM((steps, CHUNKS, 6, part, wide), BF16),
-            pltpu.VMEM((steps, CHUNKS, 6, part, wide), BF16),
+            pltpu.VMEM((CHUNKS, nodes, part, wide), F32),
+            pltpu.VMEM((steps, CHUNKS, 3, nodes, part, wide), BF16),
+            pltpu.VMEM((steps, CHUNKS, 3, nodes, part, wide), BF16),
             dma((steps + 1, CHUNKS, 2)),
             dma((steps + 1, CHUNKS, 2)),
-            dma((steps, CHUNKS, 6)),
-            dma((steps, CHUNKS, 6)),
-            dma((steps + 1, 4)),
-            dma((steps + 1, 4)),
+            dma((steps, CHUNKS, 3)),
+            dma((steps, CHUNKS, 3)),
+            dma((steps + 1, 5)),
+            dma((steps + 1, 5)),
             dma((2,)),
             dma((steps,)),
             dma((steps + 1,)),
@@ -464,7 +407,7 @@
             dma((steps, CHUNKS)),
         ],
         compiler_params=pltpu.CompilerParams(
-            collective_id=0, has_side_effects=True, vmem_limit_bytes=48 * 1024 * 1024
+            collective_id=0, has_side_effects=True, vmem_limit_bytes=62 * 1024 * 1024
         ),
         cost_estimate=pl.CostEstimate(
             flops=4_000_000_000, bytes_accessed=10_000_000, transcendentals=0

time: 134 us -> 108 us (0.81)
  Pallas kernels: 128 us -> 105 us
  local copies, waits for them, and re-layouts: 5.99 us -> 2.06 us
    pallas_call x1, Pallas kernels: 128 us -> 105 us  [on_device(): pl.pallas_call(functools.partial(kernel, sizes), out_shape=jax.ShapeDtype...]
    unnamed x11 -> x1, local copies, waits for them, and re-layouts: 5.99 us -> 2.06 us
where the time goes in v2:
time: 108 us; the launch traced here: 107 us
  Pallas kernels  105 us (97%)
  local copies, waits for them, and re-layouts  2.06 us (2%)
    pallas_call x1, Pallas kernels, on_device(): pl.pallas_call(functools.partial(kernel, sizes), out_shape=jax.ShapeDtype...  105 us

profile of v2, /device:TPU:2, one launch (start us, length us, event | category | flops | bytes accessed | tf_op | source)
XLA Modules:
  0.0 107.4 jit_solution(1513833388229124483)
XLA Ops:
  0.0 105.3 %solve.1 = bf16[6,2,64,512]{3,2,1,0:T(8,128)(2,1)} custom-call(bf16[6,2,256,512]{3,2,1,0:T(8,128)(2,1)} %right_side.1, bf16[5,2,8,64,256]{4,3,2,1,0:T(8,128)(2,1)} %lower_blocks.1, bf16[5,2,8,64,256]{4,3,2,1,0:T(8,128)(2,1)} %upper_blocks.1, bf16[6,2,64,256]{3,2,1,0:T(8,128)(2,1)} %lower_inverse.1, bf16[6,2,64,256]{3,2,1,0:T(8,128)(2,1)} %upper_inverse.1, ...), custom_call_target="tpu_custom_call" | custom-call | flops 4000000000 | bytes 10000000 | tf_op jit(solution)/shard_map/solve/pallas_call | solution.py:381
  105.3 2.1 %copy.9 = bf16[6,2,64,512]{3,2,1,0:T(8,128)(2,1)} copy(bf16[6,2,64,512]{3,2,1,0:T(8,128)(2,1)} %solve.1) | data formatting | bytes 1572864

commit v3 on v2

--- a/solution.py
+++ b/solution.py
@@ -93,34 +93,23 @@
     all_own += [load_own(t, upper_inverse, steps - t) for t in range(levels - 1, steps + 1)]
     all_extra = [load_extra(s, h) for s in range(levels - 1) for h in range(CHUNKS)]
 
+    barrier = pltpu.get_barrier_semaphore()
+    for place in peers:
+        pl.semaphore_signal(barrier, inc=1, device_id=place, device_id_type=pl.DeviceIdType.MESH)
+
+    @pl.when(has_low)
+    def _():
+        pl.semaphore_signal(barrier, inc=1, device_id=low, device_id_type=pl.DeviceIdType.MESH)
+
+    @pl.when(has_high)
+    def _():
+        pl.semaphore_signal(barrier, inc=1, device_id=high, device_id_type=pl.DeviceIdType.MESH)
+
     all_own[0].start()
     load_inverse.start()
     load_side.start()
     all_blocks[0].start()
-    for copy in all_own[1:3]:
-        copy.start()
-    for copy in all_extra[:CHUNKS]:
-        copy.start()
-    all_blocks[1].start()
-
-    barrier = pltpu.get_barrier_semaphore()
-    for place in peers:
-        pl.semaphore_signal(barrier, inc=1, device_id=place, device_id_type=pl.DeviceIdType.MESH)
-
-    @pl.when(has_low)
-    def _():
-        pl.semaphore_signal(barrier, inc=1, device_id=low, device_id_type=pl.DeviceIdType.MESH)
-
-    @pl.when(has_high)
-    def _():
-        pl.semaphore_signal(barrier, inc=1, device_id=high, device_id_type=pl.DeviceIdType.MESH)
-
-    for copy in all_own[3:]:
-        copy.start()
-    for copy in all_extra[CHUNKS:]:
-        copy.start()
-    for copy in all_blocks[2:]:
-        copy.start()
+    all_own[1].start()
 
     line = lax.broadcasted_iota(jnp.int32, (part, order), 0)
     place = lax.broadcasted_iota(jnp.int32, (part, order), 1)
@@ -136,7 +125,7 @@
 
     @pl.when(jnp.logical_not(has_high))
     def _():
-        known[:, :, 2 * nodes : 3 * nodes] = jnp.zeros((steps + 1, CHUNKS, nodes, part, wide), BF16)
+        known[:, :, nodes : 2 * nodes] = jnp.zeros((steps + 1, CHUNKS, nodes, part, wide), BF16)
 
     pl.semaphore_wait(barrier, 3 + jnp.where(has_low, 1, 0) + jnp.where(has_high, 1, 0))
 
@@ -161,8 +150,8 @@
         return remote(source, target, gather_out.at[turn, which], gather_in.at[turn, which], place)
 
     def halo_copy(step, chunk, side):
-        source = known.at[step, chunk, pl.ds(nodes, nodes)]
-        target = known.at[step, chunk, pl.ds(0 if side == 0 else 2 * nodes, nodes)]
+        source = known.at[step, chunk, pl.ds(2 * nodes, nodes)]
+        target = known.at[step, chunk, pl.ds(0 if side == 0 else nodes, nodes)]
         return remote(
             source,
             target,
@@ -182,7 +171,7 @@
 
     def result_copy(step, chunk):
         return pltpu.make_async_copy(
-            known.at[step + 1, chunk, pl.ds(nodes, nodes)],
+            known.at[step + 1, chunk, pl.ds(2 * nodes, nodes)],
             out.at[steps - 1 - step, :, :, pl.ds(chunk * wide, wide)],
             result_sem.at[step, chunk],
         )
@@ -232,6 +221,7 @@
         sources = lower_source if is_lower else upper_source
         level = step if is_lower else steps - 1 - step
         base = (row - 1) * nodes
+        spots = [*range(nodes), *range(2 * nodes, 3 * nodes), *range(nodes, 2 * nodes)]
         tile = 16
 
         def one(node):
@@ -247,7 +237,7 @@
                     total = jnp.zeros((tile, order), F32)
                     for term in range(terms):
                         total = total - jnp.where(slots[term] == slot, values[term], 0.0)
-                    inverse[node, slot, start : start + tile, :] = total.astype(BF16)
+                    inverse[node, spots[slot], start : start + tile, :] = total.astype(BF16)
 
         for node in range(nodes):
             one(node)
@@ -277,14 +267,17 @@
     def multiply(step, chunk):
         if step < levels - 1:
             load_extra(step, chunk).wait()
+        half = 2 * nodes * part
+        near = known[step, chunk, 2 * nodes :].reshape(half, wide)
+        one = dot(operator[step, 0:2, :, :, half:].reshape(half, half), near)
+        two = dot(operator[step, 2:4, :, :, half:].reshape(half, half), near)
         end_halo(step, chunk)
-        values = known[step, chunk].reshape(4 * nodes * part, wide)
-        half = 2 * nodes * part
-        one = dot(operator[step, 0:2].reshape(half, -1), values)
+        far = known[step, chunk, : 2 * nodes].reshape(half, wide)
+        one = one + dot(operator[step, 0:2, :, :, :half].reshape(half, half), far)
         sent[step, chunk, 0:2] = one.astype(BF16).reshape(2, nodes, part, wide)
         part_copy(step, chunk, 0).start()
         part_copy(step, chunk, 1).start()
-        two = dot(operator[step, 2:4].reshape(half, -1), values)
+        two = two + dot(operator[step, 2:4, :, :, :half].reshape(half, half), far)
         sent[step, chunk, 2] = two[: nodes * part].astype(BF16).reshape(nodes, part, wide)
         part_copy(step, chunk, 2).start()
         kept[chunk] = two[nodes * part :].reshape(nodes, part, wide)
@@ -296,7 +289,7 @@
         for which in range(3):
             total = total + received[step, chunk, which].astype(F32)
         value = total.astype(BF16)
-        known[step + 1, chunk, nodes : 2 * nodes] = value
+        known[step + 1, chunk, 2 * nodes : 3 * nodes] = value
         if step < steps - 1:
             start_halo(step + 1, chunk)
         if step < top:
@@ -305,6 +298,8 @@
             result_copy(step, chunk).start()
 
     start_gather(0)
+    for copy in all_extra[:CHUNKS]:
+        copy.start()
     load_inverse.wait()
     load_side.wait()
     for chunk in range(CHUNKS):
@@ -312,12 +307,15 @@
             value = dot(
                 first_inverse[node], first_side[node, :, chunk * wide : (chunk + 1) * wide]
             ).astype(BF16)
-            known[0, chunk, nodes + node] = value
+            known[0, chunk, 2 * nodes + node] = value
             known[steps - 1, chunk, 3 * nodes + node] = value
         start_halo(0, chunk)
-    relay_gather(0)
     start_gather(1)
+    for copy in (*all_own[2:4], all_blocks[1], *all_extra[CHUNKS:2 * CHUNKS]):
+        copy.start()
     make_operator(0)
+    for copy in (*all_own[4:], *all_blocks[2:], *all_extra[2 * CHUNKS:]):
+        copy.start()
 
     late = CHUNKS // 2
     for step in range(steps):

time: 108 us -> 107 us (level)
  no operation moved by 1% of the time
where the time goes in v3:
time: 107 us; the launch traced here: 106 us
  Pallas kernels  104 us (97%)
  local copies, waits for them, and re-layouts  2.06 us (2%)
    pallas_call x1, Pallas kernels, on_device(): pl.pallas_call(functools.partial(kernel, sizes), out_shape=jax.ShapeDtype...  104 us

profile of v3, /device:TPU:2, one launch (start us, length us, event | category | flops | bytes accessed | tf_op | source)
XLA Modules:
  0.0 106.4 jit_solution(5911897453592559423)
XLA Ops:
  0.0 104.3 %solve.1 = bf16[6,2,64,512]{3,2,1,0:T(8,128)(2,1)} custom-call(bf16[6,2,256,512]{3,2,1,0:T(8,128)(2,1)} %right_side.1, bf16[5,2,8,64,256]{4,3,2,1,0:T(8,128)(2,1)} %lower_blocks.1, bf16[5,2,8,64,256]{4,3,2,1,0:T(8,128)(2,1)} %upper_blocks.1, bf16[6,2,64,256]{3,2,1,0:T(8,128)(2,1)} %lower_inverse.1, bf16[6,2,64,256]{3,2,1,0:T(8,128)(2,1)} %upper_inverse.1, ...), custom_call_target="tpu_custom_call" | custom-call | flops 4000000000 | bytes 10000000 | tf_op jit(solution)/shard_map/solve/pallas_call | solution.py:379
  104.3 2.1 %copy.9 = bf16[6,2,64,512]{3,2,1,0:T(8,128)(2,1)} copy(bf16[6,2,64,512]{3,2,1,0:T(8,128)(2,1)} %solve.1) | data formatting | bytes 1572864

commit v4 on v3

--- a/solution.py
+++ b/solution.py
@@ -286,7 +286,6 @@
         total = kept[chunk]
         for which in (1, 2, 0):
             part_copy(step, chunk, which).wait_recv()
-        for which in range(3):
             total = total + received[step, chunk, which].astype(F32)
         value = total.astype(BF16)
         known[step + 1, chunk, 2 * nodes : 3 * nodes] = value

time: 107 us -> 107 us (level)
  no operation moved by 1% of the time
where the time goes in v4:
time: 107 us; the launch traced here: 106 us
  Pallas kernels  104 us (97%)
  local copies, waits for them, and re-layouts  2.06 us (2%)
    pallas_call x1, Pallas kernels, on_device(): pl.pallas_call(functools.partial(kernel, sizes), out_shape=jax.ShapeDtype...  104 us

profile of v4, /device:TPU:2, one launch (start us, length us, event | category | flops | bytes accessed | tf_op | source)
XLA Modules:
  0.0 106.5 jit_solution(8140362773100381780)
XLA Ops:
  0.0 104.4 %solve.1 = bf16[6,2,64,512]{3,2,1,0:T(8,128)(2,1)} custom-call(bf16[6,2,256,512]{3,2,1,0:T(8,128)(2,1)} %right_side.1, bf16[5,2,8,64,256]{4,3,2,1,0:T(8,128)(2,1)} %lower_blocks.1, bf16[5,2,8,64,256]{4,3,2,1,0:T(8,128)(2,1)} %upper_blocks.1, bf16[6,2,64,256]{3,2,1,0:T(8,128)(2,1)} %lower_inverse.1, bf16[6,2,64,256]{3,2,1,0:T(8,128)(2,1)} %upper_inverse.1, ...), custom_call_target="tpu_custom_call" | custom-call | flops 4000000000 | bytes 10000000 | tf_op jit(solution)/shard_map/solve/pallas_call | solution.py:378
  104.4 2.1 %copy.9 = bf16[6,2,64,512]{3,2,1,0:T(8,128)(2,1)} copy(bf16[6,2,64,512]{3,2,1,0:T(8,128)(2,1)} %solve.1) | data formatting | bytes 1572864
